TPU v7x, 512 devices: a whole 4x8x8 slice. The times are simulated.
512 devices in a mesh: cand: 64 (over y, z), tp: 8 (over x, core).
Axes of the slice: x: 4, y: 8, z: 8, core: 2. Of those that a mesh axis runs over, the one named last changes fastest.
Arguments:
- hidden_in: bfloat16 [24576, 4096], P('cand', 'tp'), may hold values from -6 to 6
- norm_gain: float32 [4096], replicated, may hold values from 0.1 to 1.9
- w_query: bfloat16 [4096, 4096], P('cand', 'tp'), may hold values from -0.09375 to 0.09375
- w_key: bfloat16 [4096, 1024], P('cand', 'tp'), may hold values from -0.09375 to 0.09375
- w_value: bfloat16 [4096, 1024], P('cand', 'tp'), may hold values from -0.09375 to 0.09375
- q_gain: float32 [128], replicated, may hold values from 0.1 to 1.9
- k_gain: float32 [128], replicated, may hold values from 0.1 to 1.9
- w_out: bfloat16 [4096, 4096], P('tp', 'cand'), may hold values from -0.25 to 0.25
- lengths: int32 [256], P('cand'), may hold values from 48 to 96, as said below
- positions: int32 [256], P('cand'), may hold values from 24 to 95, as said below
Outputs:
- attn_out: bfloat16 [24576, 4096], P('cand', 'tp')
Inputs may be any that keep to these rules, and one draw needn't show every extreme that they name: Every candidate has lengths at least 48 and at most 96, and the first candidate of every block of 4 has length 96. `positions`: each interaction slot lies inside its candidate's valid tokens, in its second half.
All inputs are finite; a program needn't handle non-finite values.
Results may differ from a plain program's by a relative error of at most 0.017.
Values may be sent and summed in bfloat16 or wider, within the bound.
A program may use at most 64 MiB of HBM per device.

v0:
```python
import jax
import jax.numpy as jnp
from jax import lax
from jax.sharding import PartitionSpec as P

HD = 128
SEQ = 96


EPSILON = 1e-06
THETA = 1000000.0


def head_norm(values, weight):
    return values * lax.rsqrt(jnp.mean(values * values, axis=-1, keepdims=True) + EPSILON) * weight


def rotate(values, cosine, sine):
    half_width = values.shape[-1] // 2
    turned = jnp.concatenate([-values[..., half_width:], values[..., :half_width]], axis=-1)
    return values * cosine + turned * sine


def rope_tables(length, width):
    half_width = width // 2
    frequency = THETA ** (-(jnp.arange(half_width, dtype=jnp.float32) * 2.0 / width))
    angles = jnp.arange(length, dtype=jnp.float32)[:, None] * frequency[None, :]
    angles = jnp.concatenate([angles, angles], axis=-1)
    return (jnp.cos(angles), jnp.sin(angles))


def attend(query, keys, vals, lengths, positions, key_all, value_all, own_index):
    length = query.shape[1]
    scale = float(query.shape[-1]) ** (-0.5)
    scores = (
        jnp.einsum("csngd,ctnd->cngst", query, keys, preferred_element_type=jnp.float32) * scale
    )
    slots = jnp.arange(length)
    causal = slots[None, :] <= slots[:, None]
    valid = slots[None, :] < lengths[:, None]
    allowed = causal[None, None, None, :, :] & valid[:, None, None, None, :]
    weights_local = jnp.where(allowed, jnp.exp(scores), 0.0)
    denom_local = jnp.sum(weights_local, axis=-1)
    pick = positions[:, None, None, None, None]
    query_int = jnp.take_along_axis(query, pick, axis=1)[:, 0]
    ext_scores = (
        jnp.einsum("cngd,end->cnge", query_int, key_all, preferred_element_type=jnp.float32) * scale
    )
    others = jnp.arange(key_all.shape[0])[None, :] != own_index[:, None]
    weights_ext = jnp.where(others[:, None, None, :], jnp.exp(ext_scores), 0.0)
    denom_ext = jnp.sum(weights_ext, axis=-1)
    onehot = (slots[None, :] == positions[:, None]).astype(jnp.float32)
    denom_at = (
        jnp.take_along_axis(denom_local, positions[:, None, None, None], axis=3)[..., 0] + denom_ext
    )
    denom = denom_local + onehot[:, None, None, :] * denom_ext[..., None]
    probs_local = (weights_local / denom[..., None]).astype(jnp.bfloat16)
    probs_ext = (weights_ext / denom_at[..., None]).astype(jnp.bfloat16)
    out_local = jnp.einsum(
        "cngst,ctnd->csngd", probs_local, vals, preferred_element_type=jnp.float32
    )
    out_ext = jnp.einsum("cnge,end->cngd", probs_ext, value_all, preferred_element_type=jnp.float32)
    mixed = out_local + onehot[:, :, None, None, None] * out_ext[:, None]
    return mixed.astype(jnp.bfloat16)


def shards(
    hidden_in, norm_gain, w_query, w_key, w_value, q_gain, k_gain, w_out, lengths, positions
):
    row_count = hidden_in.shape[0]
    cand_count = row_count // SEQ
    whole = lax.all_gather(hidden_in, "tp", axis=1, tiled=True)
    values32 = whole.astype(jnp.float32)
    inverse = lax.rsqrt(jnp.mean(values32 * values32, axis=-1, keepdims=True) + EPSILON)
    normed = (values32 * inverse * norm_gain).astype(jnp.bfloat16)
    full_query, full_key, full_value = (
        lax.all_gather(w_query, "cand", axis=0, tiled=True),
        lax.all_gather(w_key, "cand", axis=0, tiled=True),
        lax.all_gather(w_value, "cand", axis=0, tiled=True),
    )
    query = jnp.dot(normed, full_query, preferred_element_type=jnp.float32)
    keys = jnp.dot(normed, full_key, preferred_element_type=jnp.float32)
    vals = jnp.dot(normed, full_value, preferred_element_type=jnp.float32)
    kv_count = w_key.shape[1] // HD
    group_size = w_query.shape[1] // HD // kv_count
    cosine, sine = rope_tables(SEQ, HD)
    query = head_norm(query.reshape(cand_count, SEQ, kv_count, group_size, HD), q_gain)
    query = rotate(query, cosine[None, :, None, None, :], sine[None, :, None, None, :]).astype(
        jnp.bfloat16
    )
    keys = head_norm(keys.reshape(cand_count, SEQ, kv_count, HD), k_gain)
    keys = rotate(keys, cosine[None, :, None, :], sine[None, :, None, :]).astype(jnp.bfloat16)
    vals = vals.reshape(cand_count, SEQ, kv_count, HD).astype(jnp.bfloat16)
    pick = positions[:, None, None, None]
    key_int = jnp.take_along_axis(keys, pick, axis=1)[:, 0]
    value_int = jnp.take_along_axis(vals, pick, axis=1)[:, 0]
    key_all, value_all = (
        lax.all_gather(key_int, "cand", axis=0, tiled=True),
        lax.all_gather(value_int, "cand", axis=0, tiled=True),
    )
    own_index = lax.axis_index("cand") * cand_count + jnp.arange(cand_count, dtype=jnp.int32)
    mixed = attend(query, keys, vals, lengths, positions, key_all, value_all, own_index)
    mixed = mixed.reshape(row_count, w_query.shape[1])
    partial_out = jnp.dot(
        mixed, lax.all_gather(w_out, "cand", axis=1, tiled=True), preferred_element_type=jnp.float32
    )
    return lax.psum_scatter(partial_out.astype(jnp.bfloat16), "tp", scatter_dimension=1, tiled=True)


def solution(mesh):
    in_specs = (
        P("cand", "tp"),
        P(),
        P("cand", "tp"),
        P("cand", "tp"),
        P("cand", "tp"),
        P(),
        P(),
        P("tp", "cand"),
        P("cand"),
        P("cand"),
    )
    out_specs = P("cand", "tp")
    return jax.shard_map(shards, mesh=mesh, in_specs=in_specs, out_specs=out_specs, check_vma=False)
```

profile of v0, /device:TPU:1, one launch (start us, length us, event | category | flops | bytes accessed | tf_op | source)
XLA Modules:
  0.0 437.2 jit_solution(18202787386022692956)
XLA Ops:
  6.5 0.7 all-gather.8.cloned.1.call-update
  7.3 0.7 all-gather.12.cloned.1.call-update
  8.1 0.7 all-gather.10.cloned.1.call-update
  8.8 0.5 all-gather.14.cloned.1.call-update
  9.4 0.5 all-gather.16.cloned.1.call-update
  10.0 0.7 fusion.44
  10.6 0.7 fusion.47
  11.4 0.3 fusion.36
  11.6 1.3 and_bitcast_fusion
  12.9 1.2 compare_and_fusion
  14.1 0.7 iota_compare_fusion.3
  14.8 0.6 iota_compare_fusion.1
  15.4 1.3 fusion.41
  16.7 0.7 broadcast_and_fusion
  17.5 31.0 %all-gather.8.cloned.1.call-done = bf16[384,4096]{1,0:T(8,128)(2,1)} async-done(((bf16[384,512]{1,0:T(8,128)(2,1)}), bf16[384,4096]{1,0:T(8,128)(2,1)}) %all-gather.8.cloned.1.call-update) | async-done | bytes 3145744 | tf_op jit(solution)/shard_map/all_gather | solution.py:72
  48.5 2.6 fusion
  51.1 77.6 %all-gather.12.cloned.1.call-done = bf16[4096,128]{1,0:T(8,128)(2,1)} async-done(((bf16[64,128]{1,0:T(8,128)(2,1)}), bf16[4096,128]{1,0:T(8,128)(2,1)}) %all-gather.12.cloned.1.call-update) | async-done | bytes 1048592 | tf_op jit(solution)/shard_map/all_gather | solution.py:78
  128.8 3.3 multiply_reduce_fusion.1
  132.3 0.8 fusion.48
  133.1 0.8 fusion.24
  133.9 0.6 gather_fusion.2
  134.5 76.1 %all-gather.10.cloned.1.call-done = bf16[4096,128]{1,0:T(8,128)(2,1)} async-done(((bf16[64,128]{1,0:T(8,128)(2,1)}), bf16[4096,128]{1,0:T(8,128)(2,1)}) %all-gather.10.cloned.1.call-update) | async-done | bytes 1048592 | tf_op jit(solution)/shard_map/all_gather | solution.py:79
  210.7 2.3 convolution_convert_fusion.1
  213.0 0.6 gather_fusion.3
  213.6 40.3 %all-gather = bf16[256,1,1,128]{3,2,1,0:T(2,128)(2,1)} all-gather(bf16[4,1,1,128]{3,2,1,0:T(2,128)(2,1)S(1)} %copy.26), channel_id=2, replica_groups=mesh['cand'=64,'tp'=8] {'cand'}, dimensions={0}, use_global_device_ids=true | all-gather | bytes 66560 | tf_op jit(solution)/shard_map/all_gather | solution.py:98
  253.9 41.9 %all-gather.1 = bf16[256,1,1,128]{3,2,1,0:T(2,128)(2,1)} all-gather(bf16[4,1,1,128]{3,2,1,0:T(2,128)(2,1)S(1)} %copy.28), channel_id=3, replica_groups=mesh['cand'=64,'tp'=8] {'cand'}, dimensions={0}, use_global_device_ids=true | all-gather | bytes 66560 | tf_op jit(solution)/shard_map/all_gather | solution.py:99
  295.9 2.9 all-gather.14.cloned.1.call-done
  298.7 5.0 %fusion.50 = f32[384,512]{1,0:T(8,128)S(1)} fusion(bf16[4096,512]{1,0:T(8,128)(2,1)} %all-gather.14.cloned.1.call-done, bf16[384,4096]{1,0:T(8,128)(2,1)} %all-gather.8.cloned.1.call-done, f32[4096]{0:T(1024)S(1)} %copy-done.15, f32[384]{0:T(512)S(1)} %copy-done.12), kind=kOutput, calls=%fused_computation.100 | convolution fusion | flops 1616904192 | bytes 8144384 | tf_op jit(solution)/shard_map/dot_general | solution.py:81
  303.7 0.3 reshape.603
  304.0 0.3 reshape.602
  304.3 0.5 multiply_reduce_fusion
  304.9 0.5 multiply_multiply_fusion
  305.4 0.6 fusion.49
  306.0 1.0 fusion.12
  307.1 0.5 fusion.56
  307.6 0.1 copy.29
  307.7 2.4 fusion.19
  310.2 1.6 gather_fusion
  311.7 0.6 gather_fusion.1
  312.3 1.2 fusion.55
  313.5 0.7 select_add_fusion
  314.2 0.7 multiply_add_fusion
  314.9 1.1 convolution_bitcast_fusion.1
  316.0 1.2 fusion.6
  317.3 0.2 copy.30
  317.5 67.3 %all-gather.16.cloned.1.call-done = bf16[512,4096]{0,1:T(8,128)(2,1)} async-done(((bf16[512,64]{0,1:T(8,128)(2,1)}), bf16[512,4096]{0,1:T(8,128)(2,1)}) %all-gather.16.cloned.1.call-update) | async-done | bytes 4194320 | tf_op jit(solution)/shard_map/all_gather | solution.py:105
  384.7 5.7 %convolution_convert_fusion = bf16[384,4096]{1,0:T(8,128)(2,1)} fusion(bf16[512,4096]{0,1:T(8,128)(2,1)} %all-gather.16.cloned.1.call-done, bf16[48,8,4,128]{3,2,1,0:T(4,128)(2,1)S(1)} %bitcast.123), kind=kOutput, calls=%fused_computation.9 | convolution fusion | flops 1612185600 | bytes 7733248 | tf_op jit(solution)/shard_map/dot_general | solution.py:104
  390.5 39.8 %reduce-scatter.2.cloned.1.call-done = bf16[384,512]{1,0:T(8,128)(2,1)} async-done(((bf16[384,4096]{1,0:T(8,128)(2,1)}), bf16[384,512]{1,0:T(8,128)(2,1)}) %reduce-scatter.2.cloned.1.call-update) | async-done | bytes 393232 | tf_op jit(solution)/shard_map/reduce_scatter | solution.py:107
  (55 shorter events, 0.7 us)
Async XLA Ops:
  6.5 42.0 %all-gather.8.cloned.1.call-start = ((), (), s32[]{:S(2)}) async-start(), calls=%async_computation.1 | async-start | bytes 3538944 | tf_op jit(solution)/shard_map/all_gather | solution.py:72
  7.3 121.5 %all-gather.12.cloned.1.call-start = ((), (), s32[]{:S(2)}) async-start(), calls=%async_computation.3 | async-start | bytes 1064960 | tf_op jit(solution)/shard_map/all_gather | solution.py:78
  8.0 202.7 %all-gather.10.cloned.1.call-start = ((), (), s32[]{:S(2)}) async-start(), calls=%async_computation.2 | async-start | bytes 1064960 | tf_op jit(solution)/shard_map/all_gather | solution.py:79
  8.7 290.0 %all-gather.14.cloned.1.call-start = ((), (), s32[]{:S(2)}) async-start(), calls=%async_computation.4 | async-start | bytes 4259840 | tf_op jit(solution)/shard_map/all_gather | solution.py:77
  9.3 375.4 %all-gather.16.cloned.1.call-start = ((), (), s32[]{:S(2)}) async-start(), calls=%async_computation.5 | async-start | bytes 4259840 | tf_op jit(solution)/shard_map/all_gather | solution.py:105
  9.9 420.4 %reduce-scatter.2.cloned.1.call-start = ((), (), s32[]{:S(2)}) async-start(), calls=%async_computation.6 | async-start | bytes 3538944 | tf_op jit(solution)/shard_map/reduce_scatter | solution.py:107
  11.6 121.5 %copy-start.1 = (f32[96,128]{1,0:T(8,128)}, f32[96,128]{1,0:T(8,128)S(1)}, u32[]{:S(2)}) copy-start(f32[96,128]{1,0:T(8,128)S(1)} %get-tuple-element.14) | copy-start | bytes 147460
  11.6 121.5 %copy-start.3 = (f32[96,128]{1,0:T(8,128)}, f32[96,128]{1,0:T(8,128)S(1)}, u32[]{:S(2)}) copy-start(f32[96,128]{1,0:T(8,128)S(1)} %get-tuple-element.15) | copy-start | bytes 147460
  51.1 81.0 %copy-start.11 = (f32[384]{0:T(512)}, f32[384]{0:T(512)S(1)}, u32[]{:S(2)}) copy-start(f32[384]{0:T(512)S(1)} %add_rsqrt_fusion.2) | copy-start | bytes 4612
  51.1 81.1 %copy-start.8 = (f32[128]{0:T(128)S(1)}, f32[128]{0:T(128)}, u32[]{:S(2)}) copy-start(f32[128]{0:T(128)} %param.18) | copy-start | bytes 1540
  51.1 159.6 %copy-start = (bf16[384,4096]{1,0:T(8,128)(2,1)S(1)}, bf16[384,4096]{1,0:T(8,128)(2,1)}, u32[]{:S(2)}) copy-start(bf16[384,4096]{1,0:T(8,128)(2,1)} %all-gather.8.cloned.1.call-done) | copy-start | bytes 9437188
  134.5 79.0 %copy-start.14 = (pred[4]{0:T(512)(128)(4,1)S(1)}, pred[4]{0:T(512)(128)(4,1)}, u32[]{:S(2)}) copy-start(pred[4]{0:T(512)(128)(4,1)} %and_bitcast_fusion) | copy-start | bytes 16
  134.5 164.2 %copy-start.12 = (f32[384]{0:T(512)S(1)}, f32[384]{0:T(512)}, u32[]{:S(2)}) copy-start(f32[384]{0:T(512)} %copy-done.11) | copy-start | bytes 4612
  134.5 164.2 %copy-start.15 = (f32[4096]{0:T(1024)S(1)}, f32[4096]{0:T(1024)}, u32[]{:S(2)}) copy-start(f32[4096]{0:T(1024)} %param.13) | copy-start | bytes 49156
  213.0 90.8 %copy-start.13 = (bf16[384,128]{1,0:T(8,128)(2,1)}, bf16[384,128]{1,0:T(8,128)(2,1)S(1)}, u32[]{:S(2)}) copy-start(bf16[384,128]{1,0:T(8,128)(2,1)S(1)} %convolution_convert_fusion.1) | copy-start | bytes 294916
  303.7 1.1 copy-start.10
  304.3 1.7 copy-start.2
  304.3 1.7 copy-start.4
  305.3 1.7 copy-start.5
  305.4 1.7 copy-start.6
  305.4 1.7 copy-start.7
  305.4 1.7 copy-start.9
Sparse Core Ops, SparseCore 0:
  9.5 38.9 all-gather.7
  51.5 77.1 all-gather.11
  131.8 78.8 all-gather.9
  213.5 85.1 all-gather.13
  301.6 83.1 all-gather.15
  390.6 39.6 reduce-scatter.1
where the time goes:
time: 439 us; the launch traced here: 437 us
  waiting for transfers between devices  298 us (68%)
  blocking collectives  82.2 us (19%)
  matrix products  20.3 us (5%)
  other arithmetic  18.4 us (4%)
  between operations  13.8 us (3%)
    all_gather x1, waiting for transfers between devices, shards(): lax.all_gather(w_key, 'cand', axis=0, tiled=True)  77.6 us
    all_gather x1, waiting for transfers between devices, shards(): lax.all_gather(w_value, 'cand', axis=0, tiled=True)  76.1 us
    all_gather x1, waiting for transfers between devices, shards(): lax.all_gather(w_out, 'cand', axis=1, tiled=True)  67.3 us
    all_gather x1, blocking collectives, shards(): lax.all_gather(value_int, 'cand', axis=0, tiled=True)  41.9 us
    all_gather x1, blocking collectives, shards(): lax.all_gather(key_int, 'cand', axis=0, tiled=True)  40.3 us
    reduce_scatter x1, waiting for transfers between devices, shards(): lax.psum_scatter(partial_out.astype(jnp.bfloat16), 'tp', scatter_dimensio...  39.8 us
    all_gather x1, waiting for transfers between devices, shards(): whole = lax.all_gather(hidden_in, 'tp', axis=1, tiled=True)  31 us
  transfers between devices with their start and end apart: 6, of which 6 were waited for; matrix products, arithmetic and copies ran while one was open for 9% of the time, Pallas kernels for 0%

commit v1 on v0

v1 whole, which is shorter than its diff:
```python
import functools

import jax
import jax.numpy as jnp
import numpy as np
from jax import lax
from jax.experimental import pallas as pl
from jax.experimental.pallas import tpu as pltpu
from jax.sharding import PartitionSpec as P

HD = 128
SEQ = 96
EPSILON = 1e-06
THETA = 1000000.0
F32, BF16 = jnp.float32, jnp.bfloat16
MESH = pl.DeviceIdType.MESH


def rope_tables():
    half = HD // 2
    frequency = np.float32(THETA) ** (-(np.arange(half, dtype=np.float32) * np.float32(2.0 / HD)))
    angles = np.arange(SEQ, dtype=np.float32)[:, None] * frequency.astype(np.float32)[None, :]
    cosine, sine = np.cos(angles), np.sin(angles)
    return (
        np.concatenate([cosine, cosine], axis=-1).astype(np.float32),
        np.concatenate([-sine, sine], axis=-1).astype(np.float32),
    )


def ring_plan(n, halves):
    far = n // 2
    if n == 1:
        return {1: [], -1: []}
    if halves == 1:
        return {
            1: [(d, 0) for d in range(1, far + 1)],
            -1: [(d, 0) for d in range(1, n - far)],
        }
    return {
        1: [(d, k) for d in range(1, far + 1) for k in (0, 1) if d < far or k == 0],
        -1: [(d, k) for d in range(1, far + 1) for k in (1, 0) if d < far or k == 1],
    }


class Sems:
    def __init__(self, send, recv):
        self.send, self.recv, self.used = send, recv, 0

    def take(self):
        self.used += 1
        return self.used - 1


class Ring:
    def __init__(self, n, me, slot, peer, sems, halves=2):
        self.n, self.me, self.slot, self.peer, self.sems = n, me, slot, peer, sems
        self.plan = ring_plan(n, halves)
        self.ids = {(s, *m): sems.take() for s in (1, -1) for m in self.plan[s]}
        self.rounds = max(len(self.plan[1]), len(self.plan[-1]))
        self.sent = []

    def at(self, offset):
        return lax.rem(self.me + offset + self.n, self.n)

    def copy(self, place, way, dist, half):
        ref, k = self.slot(place, half), self.ids[way, dist, half]
        return pltpu.make_async_remote_copy(
            src_ref=ref,
            dst_ref=ref,
            send_sem=self.sems.send.at[k],
            recv_sem=self.sems.recv.at[k],
            device_id=self.peer(self.at(way)),
            device_id_type=MESH,
        )

    def send(self, way, dist, half):
        copy = self.copy(self.at(-way * (dist - 1)), way, dist, half)
        copy.start()
        self.sent.append(copy)

    def start(self, half=None):
        for k in range(2):
            for way in (1, -1):
                mine = [m for m in self.plan[way] if m[0] == 1]
                if k < len(mine) and half in (None, mine[k][1]):
                    self.send(way, *mine[k])

    def event(self, r):
        got = []
        for way in (1, -1):
            if r < len(self.plan[way]):
                dist, half = self.plan[way][r]
                self.copy(self.at(-way * dist), way, dist, half).wait_recv()
                if (dist + 1, half) in self.plan[way]:
                    self.send(way, dist + 1, half)
                got.append((self.at(-way * dist), half))
        return got

    def finish(self):
        for copy in self.sent:
            copy.wait_send()


class Group:
    def __init__(self, *rings):
        self.rings = rings
        self.rounds = max(r.rounds for r in rings)

    def start(self):
        for ring in self.rings:
            ring.start()

    def event(self, *which):
        for r in which:
            for ring in self.rings:
                ring.event(r)

    def all(self):
        self.event(*range(self.rounds))

    def finish(self):
        for ring in self.rings:
            ring.finish()


class ChipGather:
    def __init__(self, n, x, core, cand, buf, rows, sems):
        def slot(i, half):
            return buf.at[i * 2 + core, pl.ds(half * rows, rows)]

        self.ring = Ring(n, x, slot, lambda i: (cand, i * 2 + core), sems)
        self.sems, self.buf, self.rows = sems, buf, rows
        self.n, self.x, self.core = n, x, core
        self.other = (cand, x * 2 + 1 - core)
        self.sent, self.due = [], []

    def pass_on(self, place, half):
        k = self.sems.take()
        mine = self.buf.at[place * 2 + self.core, pl.ds(half * self.rows, self.rows)]
        theirs = self.buf.at[place * 2 + 1 - self.core, pl.ds(half * self.rows, self.rows)]

        def copy(ref):
            return pltpu.make_async_remote_copy(
                src_ref=ref,
                dst_ref=ref,
                send_sem=self.sems.send.at[k],
                recv_sem=self.sems.recv.at[k],
                device_id=self.other,
                device_id_type=MESH,
            )

        out = copy(mine)
        out.start()
        self.sent.append(out)
        self.due.append(copy(theirs))

    def start(self, half=None):
        self.ring.start(half)
        for k in (0, 1):
            if half in (None, k):
                self.pass_on(self.x, k)

    def event(self, *which):
        for r in which:
            for place, half in self.ring.event(r):
                self.pass_on(place, half)

    def arrive(self):
        for copy in self.due:
            copy.wait_recv()

    def finish(self):
        self.ring.finish()
        for copy in self.sent:
            copy.wait_send()


def dot(a, b):
    return jnp.dot(a, b, preferred_element_type=F32)


def dot_t(a, b):
    return lax.dot_general(a, b, (((1,), (1,)), ((), ())), preferred_element_type=F32)


def iota(shape, axis):
    return lax.broadcasted_iota(jnp.int32, shape, axis)


def kernel(
    sizes,
    hidden,
    gain,
    w_query,
    w_key,
    w_value,
    q_gain,
    k_gain,
    w_out,
    lengths,
    positions,
    cosine,
    sine,
    out,
    hid,
    nrm,
    bk,
    bv,
    bqa,
    bqb,
    boa,
    bob,
    tokens,
    raw,
    turned,
    kbuf,
    vbuf,
    kacc,
    qacc,
    qbuf,
    mix,
    total,
    send,
    recv,
    local,
):
    Y, Z, X, TP, cands, group = sizes
    cand, t = lax.axis_index("cand"), lax.axis_index("tp")
    y, z = cand // Z, lax.rem(cand, Z)
    x, core = t // 2, lax.rem(t, 2)
    rows = cands * SEQ
    depth = w_key.shape[0]
    width = hidden.shape[1]
    half = depth // 2
    qh = group * HD // 2
    sems = Sems(send, recv)

    fetches = [
        pltpu.make_async_copy(src, dst, local.at[i])
        for i, (src, dst) in enumerate(
            [
                (w_key, bk.at[y, z]),
                (w_value, bv.at[y, z]),
                (hidden, hid.at[t]),
                (w_query.at[:, pl.ds(0, qh)], bqa.at[y, z]),
                (w_query.at[:, pl.ds(qh, qh)], bqb.at[y, z]),
                (w_out, raw),
            ]
        )
    ]
    for fetch in fetches:
        fetch.start()

    def along_y(i):
        return (i * Z + z, t)

    def along_z(i):
        return (y * Z + i, t)

    def along_x(i):
        return (cand, i * 2 + core)

    barrier = pltpu.get_barrier_semaphore()
    near = []
    for n, me, peer in ((Y, y, along_y), (Z, z, along_z), (X, x, along_x)):
        if n > 1:
            near += [peer(lax.rem(me + 1, n)), peer(lax.rem(me + n - 1, n))]
    swap = (t * Z + z, y)
    near += [(cand, x * 2 + 1 - core), swap]
    for peer in near:
        pl.semaphore_signal(barrier, inc=1, device_id=peer, device_id_type=MESH)
    pl.semaphore_wait(barrier, len(near))

    def gather(a, b):
        def part(k):
            return pl.ds(k * half, half)

        first = Group(
            Ring(Y, y, lambda i, k: a.at[i, z, part(k)], along_y, sems),
            Ring(Z, z, lambda i, k: b.at[y, i, part(k)], along_z, sems),
        )
        second = Group(
            Ring(Z, z, lambda i, k: a.at[:, i, part(k)], along_z, sems),
            Ring(Y, y, lambda i, k: b.at[i, :, part(k)], along_y, sems),
        )
        return first, second

    K1, K2 = gather(bk, bv)
    Q1, Q2 = gather(bqa, bqb)
    O1, O2 = gather(boa, bob)
    I1 = Group(Ring(Z, z, lambda i, k: tokens.at[y, i], along_z, sems, 1))
    I2 = Group(Ring(Y, y, lambda i, k: tokens.at[i], along_y, sems, 1))
    H = ChipGather(X, x, core, cand, hid, rows // 2, sems)
    M = ChipGather(X, x, core, cand, mix, rows // 2, sems)

    fetches[0].wait()
    fetches[1].wait()
    K1.start()
    fetches[2].wait()
    H.start()
    fetches[3].wait()
    fetches[4].wait()
    Q1.start()

    fetches[5].wait()
    eye = (iota((depth, depth), 0) == iota((depth, depth), 1)).astype(F32).astype(BF16)
    flat = dot_t(eye, raw[...]).astype(BF16)
    turned[0] = flat[:, :qh]
    turned[1] = flat[:, qh:]
    swaps = [sems.take(), sems.take()]

    def swap_copy(i, place):
        return pltpu.make_async_remote_copy(
            src_ref=turned.at[i],
            dst_ref=(boa, bob)[i].at[place, z],
            send_sem=send.at[swaps[i]],
            recv_sem=recv.at[swaps[i]],
            device_id=swap,
            device_id_type=MESH,
        )

    @pl.when(t != y)
    def _():
        for i in range(2):
            swap_copy(i, t).start()

    @pl.when(t == y)
    def _():
        for i in range(2):
            (boa, bob)[i][y, z] = turned[i]

    K1.all()
    K2.start()
    H.event(*range(0, min(1, H.ring.rounds)))
    Q1.all()
    K2.event(0, 1)
    H.event(*range(1, min(2, H.ring.rounds)))
    K2.event(2, 3, 4)
    Q2.start()
    H.event(*range(2, H.ring.rounds))
    K2.event(5, 6)

    @pl.when(t != y)
    def _():
        for i in range(2):
            swap_copy(i, y).wait_recv()

    O1.start()
    H.arrive()

    def squares(i, acc):
        v = hid[i].astype(F32)
        return acc + jnp.sum(v * v, axis=-1, keepdims=True)

    square = lax.fori_loop(0, TP, squares, jnp.zeros((rows, 1), F32))
    inverse = lax.rsqrt(square * (1.0 / (TP * width)) + EPSILON)

    def scale(i, carry):
        lanes = pl.ds(pl.multiple_of(i * width, 128), width)
        nrm[:, lanes] = (hid[i].astype(F32) * inverse * gain[:, lanes]).astype(BF16)
        return carry

    Q2.event(0)
    lax.fori_loop(0, TP, scale, 0)
    O1.event(0)
    Q2.event(1)

    def norm_rope(v, weight):
        v = v * lax.rsqrt(jnp.mean(v * v, axis=-1, keepdims=True) + EPSILON) * weight
        return (v * cosine[...] + pltpu.roll(v, HD // 2, 1) * sine[...]).astype(BF16)

    kacc[:, :HD] = dot(nrm[...], bk[...].reshape(TP * width, HD))
    kacc[:, HD:] = dot(nrm[...], bv[...].reshape(TP * width, HD))
    O1.event(1)
    Q2.event(2)
    pad = jnp.zeros((HD - SEQ, HD), BF16)
    picked = jnp.zeros((16, HD), F32)
    for j in range(cands):
        span = pl.ds(j * SEQ, SEQ)
        kj = norm_rope(kacc[span, :HD], k_gain[...])
        vj = kacc[span, HD:].astype(BF16)
        kbuf[j] = jnp.concatenate([kj, pad], axis=0)
        vbuf[j] = jnp.concatenate([vj, pad], axis=0)
        here = iota((16, HD), 1) == positions[j]
        for at, block in ((j, kbuf), (cands + j, vbuf)):
            sel = jnp.where(here & (iota((16, HD), 0) == at), 1.0, 0.0).astype(BF16)
            picked += dot(sel, block[j])
    tokens[y, z] = picked.astype(BF16)
    I1.start()
    O1.event(2)
    I1.event(0)
    Q2.event(3)
    I1.event(1)
    O1.event(3)
    I1.event(2)
    Q2.event(4)
    I1.event(3)
    I2.start()
    O1.event(4, 5)
    I2.event(0)
    Q2.event(5)
    I2.event(1)
    O1.event(6)
    O2.start()
    I2.event(2)
    Q2.event(6)

    qacc[:, :qh] = dot(nrm[...], bqa[...].reshape(TP * width, qh))
    I2.event(3)
    O2.event(0)
    qacc[:, qh:] = dot(nrm[...], bqb[...].reshape(TP * width, qh))
    asked = jnp.zeros((16, HD), F32)
    for j in range(cands):
        for h in range(group):
            qbuf[j, pl.ds(h * SEQ, SEQ)] = norm_rope(
                qacc[pl.ds(j * SEQ, SEQ), pl.ds(h * HD, HD)], q_gain[...]
            )
        shape = (16, group * SEQ)
        h = iota(shape, 0) - group * j
        here = (h >= 0) & (h < group) & (iota(shape, 1) == h * SEQ + positions[j])
        asked += dot(jnp.where(here, 1.0, 0.0).astype(BF16), qbuf[j])
    O2.event(1)

    factor = float(HD) ** (-0.5)
    flat = tokens[...].reshape(Y * Z * 16, HD)
    shape = (16, Y * Z * 16)
    column, row = iota(shape, 1), iota(shape, 0)
    inner = column & 15
    theirs = lax.shift_right_logical(column, 4) * cands + inner
    own = cand * cands + lax.div(row, jnp.int32(group))
    far = jnp.where(
        (inner < cands) & (theirs != own), jnp.exp(dot_t(asked.astype(BF16), flat) * factor), 0.0
    )
    far_den = jnp.sum(far, axis=-1, keepdims=True)
    far_sum = dot(pltpu.roll(far, cands, 1).astype(BF16), flat)

    slot_s, slot_t = iota((SEQ, HD), 0), iota((SEQ, HD), 1)
    for j in range(cands):
        allowed = (slot_t <= slot_s) & (slot_t < lengths[j])
        allowed = jnp.concatenate([allowed.astype(F32)] * group, axis=0) > 0.0
        scores = dot_t(qbuf[j], kbuf[j]) * factor
        e = jnp.where(allowed, jnp.exp(scores), 0.0)
        den = jnp.sum(e, axis=-1, keepdims=True)
        num = dot(e.astype(BF16), vbuf[j])
        for h in range(group):
            span = slice(h * SEQ, (h + 1) * SEQ)
            r = group * j + h
            here = slot_s == positions[j]
            d = den[span] + jnp.where(here, far_den[r : r + 1], 0.0)
            v = num[span] + jnp.where(here, far_sum[r : r + 1], 0.0)
            mix[t, pl.ds(j * SEQ, SEQ), pl.ds(h * HD, HD)] = (v / d).astype(BF16)
        if j == cands // 2 - 1:
            M.start(0)
            O2.event(2)
    M.start(1)
    O2.event(3)
    M.event(*range(0, min(1, M.ring.rounds)))
    O2.event(4)
    M.event(*range(1, min(2, M.ring.rounds)))
    O2.event(5)
    M.event(*range(2, M.ring.rounds))
    O2.event(6)
    M.arrive()

    total[...] = jnp.zeros_like(total)

    def project(i, carry):
        left = dot_t(mix[i, :, :qh], boa[i].reshape(width, qh))
        total[...] += left + dot_t(mix[i, :, qh:], bob[i].reshape(width, qh))
        return carry

    lax.fori_loop(0, TP, project, 0)
    out[...] = total[...].astype(BF16)

    for chain in (K1, K2, Q1, Q2, O1, O2, I1, I2, H, M):
        chain.finish()

    @pl.when(t != y)
    def _():
        for i in range(2):
            swap_copy(i, t).wait_send()


N_SEMS = 256


def shards(
    hidden_in, norm_gain, w_query, w_key, w_value, q_gain, k_gain, w_out, lengths, positions
):
    TP = lax.axis_size("tp")
    Y, Z, X = TP, lax.axis_size("cand") // TP, TP // 2
    rows, width = hidden_in.shape
    depth = w_key.shape[0]
    cands, group = rows // SEQ, w_query.shape[1] // w_key.shape[1]
    qh = group * HD // 2
    cosine, sine = rope_tables()
    any_, vmem, smem = (
        pl.BlockSpec(memory_space=m) for m in (pl.ANY, pltpu.VMEM, pltpu.SMEM)
    )
    return pl.pallas_call(
        functools.partial(kernel, (Y, Z, X, TP, cands, group)),
        out_shape=jax.ShapeDtypeStruct((rows, width), BF16),
        in_specs=[any_, vmem, any_, any_, any_, vmem, vmem, any_, smem, smem, vmem, vmem],
        out_specs=vmem,
        scratch_shapes=[
            pltpu.VMEM((TP, rows, width), BF16),
            pltpu.VMEM((rows, TP * width), BF16),
            pltpu.VMEM((Y, Z, depth, HD), BF16),
            pltpu.VMEM((Y, Z, depth, HD), BF16),
            pltpu.VMEM((Y, Z, depth, qh), BF16),
            pltpu.VMEM((Y, Z, depth, qh), BF16),
            pltpu.VMEM((Y, Z, depth, qh), BF16),
            pltpu.VMEM((Y, Z, depth, qh), BF16),
            pltpu.VMEM((Y, Z, 16, HD), BF16),
            pltpu.VMEM(w_out.shape, BF16),
            pltpu.VMEM((2, depth, qh), BF16),
            pltpu.VMEM((cands, HD, HD), BF16),
            pltpu.VMEM((cands, HD, HD), BF16),
            pltpu.VMEM((rows, 2 * HD), F32),
            pltpu.VMEM((rows, group * HD), F32),
            pltpu.VMEM((cands, group * SEQ, HD), BF16),
            pltpu.VMEM((TP, rows, group * HD), BF16),
            pltpu.VMEM((rows, width), F32),
            pltpu.SemaphoreType.DMA((N_SEMS,)),
            pltpu.SemaphoreType.DMA((N_SEMS,)),
            pltpu.SemaphoreType.DMA((6,)),
        ],
        compiler_params=pltpu.CompilerParams(
            collective_id=0, has_side_effects=True, vmem_limit_bytes=56 * 1024 * 1024
        ),
        cost_estimate=pl.CostEstimate(flops=4 * 10**9, bytes_accessed=2 * 10**6, transcendentals=10**6),
    )(
        hidden_in,
        norm_gain[None],
        w_query,
        w_key,
        w_value,
        q_gain[None],
        k_gain[None],
        w_out,
        lengths,
        positions,
        jnp.asarray(cosine),
        jnp.asarray(sine),
    )


def solution(mesh):
    in_specs = (
        P("cand", "tp"),
        P(),
        P("cand", "tp"),
        P("cand", "tp"),
        P("cand", "tp"),
        P(),
        P(),
        P("tp", "cand"),
        P("cand"),
        P("cand"),
    )
    out_specs = P("cand", "tp")
    return jax.shard_map(shards, mesh=mesh, in_specs=in_specs, out_specs=out_specs, check_vma=False)
```

time: 439 us -> 119 us (0.27)
  waiting for transfers between devices: 298 us -> 0 us
  Pallas kernels: 0 us -> 115 us
  blocking collectives: 82.2 us -> 0 us
  matrix products: 20.3 us -> 0 us
  other arithmetic: 18.4 us -> 0 us
  between operations: 13.8 us -> 0.01 us
    all_gather x5 -> x0, waiting for transfers between devices: 255 us -> none  [the longest x1 77.6 us: shards(): lax.all_gather(w_key, 'cand', axis=0, tiled=True)]
    pallas_call x0 -> x1, Pallas kernels: none -> 115 us  [shards(): pl.pallas_call(functools.partial(kernel, (Y, Z, X, TP, cands, group)), ou...]
    all_gather x2 -> x0, blocking collectives: 82.2 us -> none  [the longest x1 41.9 us: shards(): lax.all_gather(value_int, 'cand', axis=0, tiled=True)]
    reduce_scatter x1 -> x0, waiting for transfers between devices: 39.8 us -> none  [shards(): lax.psum_scatter(partial_out.astype(jnp.bfloat16), 'tp', scatter_dimensio...]
    dot_general x8 -> x0, matrix products: 20.3 us -> none  [the longest x1 5.7 us: shards(): jnp.dot(mixed, lax.all_gather(w_out, 'cand', axis=1, tiled=True), preferr...]
    convert_element_type x3 -> x0, other arithmetic: 4.74 us -> none  [the longest x2 3.44 us: shards(): rotate(query, cosine[None, :, None, None, :], sine[None, :, None, None, :])]
  transfers between devices with their start and end apart: 6 -> 0, of which waited for: 6 -> 0; matrix products, arithmetic and copies ran while one was open for 9% -> 0% of each run, Pallas kernels for 0% -> 0%
where the time goes in v1:
time: 119 us
  Pallas kernels  115 us (97%)
  local copies, waits for them, and re-layouts  3.37 us (3%)
    pallas_call x1, Pallas kernels, shards(): pl.pallas_call(functools.partial(kernel, (Y, Z, X, TP, cands, group)), ou...  115 us
    unnamed x2, local copies, waits for them, and re-layouts  3.37 us

profile of v1, /device:TPU:1, one launch (start us, length us, event | category | flops | bytes accessed | tf_op | source)
XLA Modules:
  0.0 118.7 jit_solution(18051261811053546355)
XLA Ops:
  0.0 1.6 %copy.13.w_out = bf16[512,64]{1,0:T(8,128)(2,1)} copy(bf16[512,64]{0,1:T(8,128)(2,1)} %param.19) | data formatting | bytes 131072 | tf_op args[7]
  1.6 115.3 %shard_map.118 = bf16[384,512]{1,0:T(8,128)(2,1)} custom-call(bf16[384,512]{1,0:T(8,128)(2,1)} %hidden.1, f32[1,4096]{1,0:T(1,128)} %bitcast.3, bf16[64,512]{1,0:T(8,128)(2,1)} %w_query.1, bf16[64,128]{1,0:T(8,128)(2,1)} %w_key.1, bf16[64,128]{1,0:T(8,128)(2,1)} %w_value.1, f32[1,128]{1,0:T(1,128)} %bitcast.4, f32[1,128]{1,0:T(1,128)} %bitcast.5, ...), custom_call_target="tpu_custom_call" | custom-call | flops 4000000000 | bytes 2000000 | tf_op jit(solution)/shard_map/pallas_call | solution.py:500
  116.9 1.8 %copy.15 = bf16[384,512]{1,0:T(8,128)(2,1)} copy(bf16[384,512]{1,0:T(8,128)(2,1)} %shard_map.118) | data formatting | bytes 786432

commit v2 on v1

--- a/solution.py
+++ b/solution.py
@@ -104,7 +104,7 @@
 class Group:
     def __init__(self, *rings):
         self.rings = rings
-        self.rounds = max(r.rounds for r in rings)
+        self.rounds = max(getattr(r, "rounds", 0) for r in rings)
 
     def start(self):
         for ring in self.rings:
@@ -118,9 +118,46 @@
     def all(self):
         self.event(*range(self.rounds))
 
+    def arrive(self):
+        for ring in self.rings:
+            ring.arrive()
+
     def finish(self):
         for ring in self.rings:
             ring.finish()
+
+
+class Direct:
+    def __init__(self, n, me, slot, peer, sems):
+        self.n, self.me, self.slot, self.peer, self.sems = n, me, slot, peer, sems
+        self.order = sorted(range(1, n), key=lambda d: (min(d, n - d), d))
+        self.ids = {d: sems.take() for d in self.order}
+        self.sent = []
+
+    def copy(self, dist, place):
+        ref = self.slot(place)
+        return pltpu.make_async_remote_copy(
+            src_ref=ref,
+            dst_ref=ref,
+            send_sem=self.sems.send.at[self.ids[dist]],
+            recv_sem=self.sems.recv.at[self.ids[dist]],
+            device_id=self.peer(lax.rem(self.me + dist, self.n)),
+            device_id_type=MESH,
+        )
+
+    def start(self):
+        for dist in reversed(self.order):
+            copy = self.copy(dist, self.me)
+            copy.start()
+            self.sent.append(copy)
+
+    def arrive(self):
+        for dist in self.order:
+            self.copy(dist, lax.rem(self.me - dist + self.n, self.n)).wait_recv()
+
+    def finish(self):
+        for copy in self.sent:
+            copy.wait_send()
 
 
 class ChipGather:
@@ -212,7 +249,6 @@
     bob,
     tokens,
     raw,
-    turned,
     kbuf,
     vbuf,
     kacc,
@@ -262,34 +298,41 @@
 
     barrier = pltpu.get_barrier_semaphore()
     near = []
-    for n, me, peer in ((Y, y, along_y), (Z, z, along_z), (X, x, along_x)):
-        if n > 1:
-            near += [peer(lax.rem(me + 1, n)), peer(lax.rem(me + n - 1, n))]
+    for n, me, peer in ((Y, y, along_y), (Z, z, along_z)):
+        near += [peer(lax.rem(me + i, n)) for i in range(1, n)]
+    if X > 1:
+        near += [along_x(lax.rem(x + 1, X)), along_x(lax.rem(x + X - 1, X))]
     swap = (t * Z + z, y)
     near += [(cand, x * 2 + 1 - core), swap]
     for peer in near:
         pl.semaphore_signal(barrier, inc=1, device_id=peer, device_id_type=MESH)
     pl.semaphore_wait(barrier, len(near))
 
-    def gather(a, b):
+    def gather(a, b, direct):
         def part(k):
             return pl.ds(k * half, half)
 
-        first = Group(
-            Ring(Y, y, lambda i, k: a.at[i, z, part(k)], along_y, sems),
-            Ring(Z, z, lambda i, k: b.at[y, i, part(k)], along_z, sems),
-        )
+        if direct:
+            first = Group(
+                Direct(Y, y, lambda i: a.at[i, z], along_y, sems),
+                Direct(Z, z, lambda i: b.at[y, i], along_z, sems),
+            )
+        else:
+            first = Group(
+                Ring(Y, y, lambda i, k: a.at[i, z, part(k)], along_y, sems),
+                Ring(Z, z, lambda i, k: b.at[y, i, part(k)], along_z, sems),
+            )
         second = Group(
             Ring(Z, z, lambda i, k: a.at[:, i, part(k)], along_z, sems),
             Ring(Y, y, lambda i, k: b.at[i, :, part(k)], along_y, sems),
         )
         return first, second
 
-    K1, K2 = gather(bk, bv)
-    Q1, Q2 = gather(bqa, bqb)
-    O1, O2 = gather(boa, bob)
-    I1 = Group(Ring(Z, z, lambda i, k: tokens.at[y, i], along_z, sems, 1))
-    I2 = Group(Ring(Y, y, lambda i, k: tokens.at[i], along_y, sems, 1))
+    K1, K2 = gather(bk, bv, True)
+    Q1, Q2 = gather(bqa, bqb, True)
+    O1, O2 = gather(boa, bob, False)
+    I1 = Direct(Z, z, lambda i: tokens.at[y, i], along_z, sems)
+    I2 = Direct(Y, y, lambda i: tokens.at[i], along_y, sems)
     H = ChipGather(X, x, core, cand, hid, rows // 2, sems)
     M = ChipGather(X, x, core, cand, mix, rows // 2, sems)
 
@@ -303,15 +346,11 @@
     Q1.start()
 
     fetches[5].wait()
-    eye = (iota((depth, depth), 0) == iota((depth, depth), 1)).astype(F32).astype(BF16)
-    flat = dot_t(eye, raw[...]).astype(BF16)
-    turned[0] = flat[:, :qh]
-    turned[1] = flat[:, qh:]
     swaps = [sems.take(), sems.take()]
 
     def swap_copy(i, place):
         return pltpu.make_async_remote_copy(
-            src_ref=turned.at[i],
+            src_ref=raw.at[:, pl.ds(i * qh, qh)],
             dst_ref=(boa, bob)[i].at[place, z],
             send_sem=send.at[swaps[i]],
             recv_sem=recv.at[swaps[i]],
@@ -327,25 +366,30 @@
     @pl.when(t == y)
     def _():
         for i in range(2):
-            (boa, bob)[i][y, z] = turned[i]
-
-    K1.all()
+            (boa, bob)[i][y, z] = raw[:, pl.ds(i * qh, qh)]
+
+    def steps(gather, r):
+        if r < gather.ring.rounds:
+            gather.event(r)
+
+    K1.arrive()
     K2.start()
-    H.event(*range(0, min(1, H.ring.rounds)))
-    Q1.all()
+    steps(H, 0)
+    Q1.arrive()
     K2.event(0, 1)
-    H.event(*range(1, min(2, H.ring.rounds)))
-    K2.event(2, 3, 4)
-    Q2.start()
-    H.event(*range(2, H.ring.rounds))
-    K2.event(5, 6)
 
     @pl.when(t != y)
     def _():
         for i in range(2):
             swap_copy(i, y).wait_recv()
 
+    steps(H, 1)
+    K2.event(2)
+    Q2.start()
+    K2.event(3, 4)
+    steps(H, 2)
     O1.start()
+    K2.event(5)
     H.arrive()
 
     def squares(i, acc):
@@ -360,10 +404,10 @@
         nrm[:, lanes] = (hid[i].astype(F32) * inverse * gain[:, lanes]).astype(BF16)
         return carry
 
+    K2.event(6)
+    lax.fori_loop(0, TP, scale, 0)
     Q2.event(0)
-    lax.fori_loop(0, TP, scale, 0)
     O1.event(0)
-    Q2.event(1)
 
     def norm_rope(v, weight):
         v = v * lax.rsqrt(jnp.mean(v * v, axis=-1, keepdims=True) + EPSILON) * weight
@@ -371,8 +415,8 @@
 
     kacc[:, :HD] = dot(nrm[...], bk[...].reshape(TP * width, HD))
     kacc[:, HD:] = dot(nrm[...], bv[...].reshape(TP * width, HD))
-    O1.event(1)
-    Q2.event(2)
+    Q2.event(1)
+    O1.event(1, 2)
     pad = jnp.zeros((HD - SEQ, HD), BF16)
     picked = jnp.zeros((16, HD), F32)
     for j in range(cands):
@@ -387,26 +431,17 @@
             picked += dot(sel, block[j])
     tokens[y, z] = picked.astype(BF16)
     I1.start()
-    O1.event(2)
-    I1.event(0)
+    Q2.event(2)
+    O1.event(3, 4, 5, 6)
     Q2.event(3)
-    I1.event(1)
-    O1.event(3)
-    I1.event(2)
+    I1.arrive()
+    I2.start()
     Q2.event(4)
-    I1.event(3)
-    I2.start()
-    O1.event(4, 5)
-    I2.event(0)
+    O2.start()
     Q2.event(5)
-    I2.event(1)
-    O1.event(6)
-    O2.start()
-    I2.event(2)
     Q2.event(6)
 
     qacc[:, :qh] = dot(nrm[...], bqa[...].reshape(TP * width, qh))
-    I2.event(3)
     O2.event(0)
     qacc[:, qh:] = dot(nrm[...], bqb[...].reshape(TP * width, qh))
     asked = jnp.zeros((16, HD), F32)
@@ -420,6 +455,7 @@
         here = (h >= 0) & (h < group) & (iota(shape, 1) == h * SEQ + positions[j])
         asked += dot(jnp.where(here, 1.0, 0.0).astype(BF16), qbuf[j])
     O2.event(1)
+    I2.arrive()
 
     factor = float(HD) ** (-0.5)
     flat = tokens[...].reshape(Y * Z * 16, HD)
@@ -454,11 +490,11 @@
             O2.event(2)
     M.start(1)
     O2.event(3)
-    M.event(*range(0, min(1, M.ring.rounds)))
+    steps(M, 0)
     O2.event(4)
-    M.event(*range(1, min(2, M.ring.rounds)))
+    steps(M, 1)
     O2.event(5)
-    M.event(*range(2, M.ring.rounds))
+    steps(M, 2)
     O2.event(6)
     M.arrive()
 
@@ -512,8 +548,7 @@
             pltpu.VMEM((Y, Z, depth, qh), BF16),
             pltpu.VMEM((Y, Z, depth, qh), BF16),
             pltpu.VMEM((Y, Z, 16, HD), BF16),
-            pltpu.VMEM(w_out.shape, BF16),
-            pltpu.VMEM((2, depth, qh), BF16),
+            pltpu.VMEM((depth, 2 * qh), BF16),
             pltpu.VMEM((cands, HD, HD), BF16),
             pltpu.VMEM((cands, HD, HD), BF16),
             pltpu.VMEM((rows, 2 * HD), F32),
@@ -537,7 +572,7 @@
         w_value,
         q_gain[None],
         k_gain[None],
-        w_out,
+        w_out.T,
         lengths,
         positions,
         jnp.asarray(cosine),

time: 119 us -> 106 us (0.89)
  Pallas kernels: 115 us -> 104 us
  local copies, waits for them, and re-layouts: 3.37 us -> 1.77 us
    pallas_call x1, Pallas kernels: 115 us -> 104 us  [shards(): pl.pallas_call(functools.partial(kernel, (Y, Z, X, TP, cands, group)), ou...]
    unnamed x2 -> x1, local copies, waits for them, and re-layouts: 3.37 us -> 1.77 us
where the time goes in v2:
time: 106 us
  Pallas kernels  104 us (98%)
  local copies, waits for them, and re-layouts  1.77 us (2%)
    pallas_call x1, Pallas kernels, shards(): pl.pallas_call(functools.partial(kernel, (Y, Z, X, TP, cands, group)), ou...  104 us

profile of v2, /device:TPU:1, one launch (start us, length us, event | category | flops | bytes accessed | tf_op | source)
XLA Modules:
  0.0 105.6 jit_solution(11625972544530618870)
XLA Ops:
  0.0 103.9 %shard_map.118 = bf16[384,512]{1,0:T(8,128)(2,1)} custom-call(bf16[384,512]{1,0:T(8,128)(2,1)} %hidden.1, f32[1,4096]{1,0:T(1,128)} %bitcast.5, bf16[64,512]{1,0:T(8,128)(2,1)} %w_query.1, bf16[64,128]{1,0:T(8,128)(2,1)} %w_key.1, bf16[64,128]{1,0:T(8,128)(2,1)} %w_value.1, f32[1,128]{1,0:T(1,128)} %bitcast.6, f32[1,128]{1,0:T(1,128)} %bitcast.7, ...), custom_call_target="tpu_custom_call" | custom-call | flops 4000000000 | bytes 2000000 | tf_op jit(solution)/shard_map/pallas_call | solution.py:536
  103.9 1.8 %copy.14 = bf16[384,512]{1,0:T(8,128)(2,1)} copy(bf16[384,512]{1,0:T(8,128)(2,1)} %shard_map.118) | data formatting | bytes 786432

commit v3 on v2

--- a/solution.py
+++ b/solution.py
@@ -247,7 +247,10 @@
     bqb,
     boa,
     bob,
-    tokens,
+    key_row,
+    value_row,
+    key_all,
+    value_all,
     raw,
     kbuf,
     vbuf,
@@ -256,6 +259,8 @@
     qbuf,
     mix,
     total,
+    near_den,
+    near_sum,
     send,
     recv,
     local,
@@ -293,17 +298,16 @@
     def along_z(i):
         return (y * Z + i, t)
 
-    def along_x(i):
-        return (cand, i * 2 + core)
+    def along_tp(i):
+        return (cand, i)
 
     barrier = pltpu.get_barrier_semaphore()
     near = []
     for n, me, peer in ((Y, y, along_y), (Z, z, along_z)):
         near += [peer(lax.rem(me + i, n)) for i in range(1, n)]
-    if X > 1:
-        near += [along_x(lax.rem(x + 1, X)), along_x(lax.rem(x + X - 1, X))]
+    near += [along_tp(lax.rem(t + i, TP)) for i in range(1, TP)]
     swap = (t * Z + z, y)
-    near += [(cand, x * 2 + 1 - core), swap]
+    near.append(swap)
     for peer in near:
         pl.semaphore_signal(barrier, inc=1, device_id=peer, device_id_type=MESH)
     pl.semaphore_wait(barrier, len(near))
@@ -331,9 +335,16 @@
     K1, K2 = gather(bk, bv, True)
     Q1, Q2 = gather(bqa, bqb, True)
     O1, O2 = gather(boa, bob, False)
-    I1 = Direct(Z, z, lambda i: tokens.at[y, i], along_z, sems)
-    I2 = Direct(Y, y, lambda i: tokens.at[i], along_y, sems)
+    I1 = Group(
+        Direct(Z, z, lambda i: key_row.at[i], along_z, sems),
+        Direct(Y, y, lambda i: value_row.at[i], along_y, sems),
+    )
+    I2 = Group(
+        Direct(Y, y, lambda i: key_all.at[i], along_y, sems),
+        Direct(Z, z, lambda i: value_all.at[i], along_z, sems),
+    )
     H = ChipGather(X, x, core, cand, hid, rows // 2, sems)
+    T = Direct(TP, t, lambda i: mix.at[i, pl.ds(rows, 16)], along_tp, sems)
     M = ChipGather(X, x, core, cand, mix, rows // 2, sems)
 
     fetches[0].wait()
@@ -418,7 +429,7 @@
     Q2.event(1)
     O1.event(1, 2)
     pad = jnp.zeros((HD - SEQ, HD), BF16)
-    picked = jnp.zeros((16, HD), F32)
+    picked = [jnp.zeros((16, HD), F32)] * 2
     for j in range(cands):
         span = pl.ds(j * SEQ, SEQ)
         kj = norm_rope(kacc[span, :HD], k_gain[...])
@@ -426,20 +437,23 @@
         kbuf[j] = jnp.concatenate([kj, pad], axis=0)
         vbuf[j] = jnp.concatenate([vj, pad], axis=0)
         here = iota((16, HD), 1) == positions[j]
-        for at, block in ((j, kbuf), (cands + j, vbuf)):
-            sel = jnp.where(here & (iota((16, HD), 0) == at), 1.0, 0.0).astype(BF16)
-            picked += dot(sel, block[j])
-    tokens[y, z] = picked.astype(BF16)
+        sel = jnp.where(here & (iota((16, HD), 0) == j), 1.0, 0.0).astype(BF16)
+        picked = [p + dot(sel, block[j]) for p, block in zip(picked, (kbuf, vbuf))]
+    key_row[z] = picked[0].astype(BF16)
+    value_row[y] = picked[1].astype(BF16)
     I1.start()
     Q2.event(2)
     O1.event(3, 4, 5, 6)
-    Q2.event(3)
+    Q2.event(3, 4)
+    O2.start()
+    Q2.event(5, 6)
     I1.arrive()
+    for n, me, rows_of, block in ((Z, y, key_row, key_all), (Y, z, value_row, value_all)):
+        shape = (n * cands, n * 16)
+        r, c = iota(shape, 0), iota(shape, 1)
+        sel = jnp.where(c == lax.div(r, jnp.int32(cands)) * 16 + lax.rem(r, jnp.int32(cands)), 1.0, 0.0)
+        block[me] = dot(sel.astype(BF16), rows_of[...].reshape(n * 16, HD)).astype(BF16)
     I2.start()
-    Q2.event(4)
-    O2.start()
-    Q2.event(5)
-    Q2.event(6)
 
     qacc[:, :qh] = dot(nrm[...], bqa[...].reshape(TP * width, qh))
     O2.event(0)
@@ -455,21 +469,8 @@
         here = (h >= 0) & (h < group) & (iota(shape, 1) == h * SEQ + positions[j])
         asked += dot(jnp.where(here, 1.0, 0.0).astype(BF16), qbuf[j])
     O2.event(1)
-    I2.arrive()
 
     factor = float(HD) ** (-0.5)
-    flat = tokens[...].reshape(Y * Z * 16, HD)
-    shape = (16, Y * Z * 16)
-    column, row = iota(shape, 1), iota(shape, 0)
-    inner = column & 15
-    theirs = lax.shift_right_logical(column, 4) * cands + inner
-    own = cand * cands + lax.div(row, jnp.int32(group))
-    far = jnp.where(
-        (inner < cands) & (theirs != own), jnp.exp(dot_t(asked.astype(BF16), flat) * factor), 0.0
-    )
-    far_den = jnp.sum(far, axis=-1, keepdims=True)
-    far_sum = dot(pltpu.roll(far, cands, 1).astype(BF16), flat)
-
     slot_s, slot_t = iota((SEQ, HD), 0), iota((SEQ, HD), 1)
     for j in range(cands):
         allowed = (slot_t <= slot_s) & (slot_t < lengths[j])
@@ -478,25 +479,50 @@
         e = jnp.where(allowed, jnp.exp(scores), 0.0)
         den = jnp.sum(e, axis=-1, keepdims=True)
         num = dot(e.astype(BF16), vbuf[j])
+        here = slot_s == positions[j]
         for h in range(group):
             span = slice(h * SEQ, (h + 1) * SEQ)
             r = group * j + h
-            here = slot_s == positions[j]
-            d = den[span] + jnp.where(here, far_den[r : r + 1], 0.0)
-            v = num[span] + jnp.where(here, far_sum[r : r + 1], 0.0)
-            mix[t, pl.ds(j * SEQ, SEQ), pl.ds(h * HD, HD)] = (v / d).astype(BF16)
+            near_den[r : r + 1] = jnp.sum(jnp.where(here, den[span], 0.0), axis=0, keepdims=True)
+            near_sum[r : r + 1] = jnp.sum(jnp.where(here, num[span], 0.0), axis=0, keepdims=True)
+            mix[t, pl.ds(j * SEQ, SEQ), pl.ds(h * HD, HD)] = (num[span] / den[span]).astype(BF16)
         if j == cands // 2 - 1:
             M.start(0)
-            O2.event(2)
     M.start(1)
+    O2.event(2)
     O2.event(3)
     steps(M, 0)
     O2.event(4)
+    I2.arrive()
+
+    count = Y * Z * cands
+    r, c = iota((count, count), 0), iota((count, count), 1)
+    inner = lax.rem(r, jnp.int32(cands))
+    there = lax.div(r, jnp.int32(cands))
+    there = (lax.rem(there, jnp.int32(Y)) * Z + lax.div(there, jnp.int32(Y))) * cands + inner
+    order = jnp.where(c == there, 1.0, 0.0).astype(BF16)
+    flat = dot(order, key_all[...].reshape(count, HD)).astype(BF16)
+    r, c = iota((16, count), 0), iota((16, count), 1)
+    there = lax.div(c, jnp.int32(cands))
+    there = (lax.rem(there, jnp.int32(Y)) * Z + lax.div(there, jnp.int32(Y))) * cands + lax.rem(
+        c, jnp.int32(cands)
+    )
+    own = cand * cands + lax.div(r, jnp.int32(group))
+    far = jnp.where(there != own, jnp.exp(dot_t(asked.astype(BF16), flat) * factor), 0.0)
+    den = near_den[...] + jnp.sum(far, axis=-1, keepdims=True)
+    num = near_sum[...] + dot(far.astype(BF16), value_all[...].reshape(count, HD))
+    mixed = (num / den).astype(BF16)
+    row, column = iota((16, 16), 0), iota((16, 16), 1)
+    for h in range(group):
+        sel = jnp.where((row < cands) & (column == row * group + h), 1.0, 0.0).astype(BF16)
+        mix[t, pl.ds(rows, 16), pl.ds(h * HD, HD)] = dot(sel, mixed).astype(BF16)
+    T.start()
     steps(M, 1)
     O2.event(5)
     steps(M, 2)
     O2.event(6)
     M.arrive()
+    T.arrive()
 
     total[...] = jnp.zeros_like(total)
 
@@ -505,10 +531,20 @@
         total[...] += left + dot_t(mix[i, :, qh:], bob[i].reshape(width, qh))
         return carry
 
-    lax.fori_loop(0, TP, project, 0)
-    out[...] = total[...].astype(BF16)
-
-    for chain in (K1, K2, Q1, Q2, O1, O2, I1, I2, H, M):
+    for n in range(2):
+        cols = slice(n * Z // 2, (n + 1) * Z // 2)
+        acc = None
+        for i in range(TP):
+            for k, buf in enumerate((boa, bob)):
+                term = dot_t(mix[i, :, k * qh : (k + 1) * qh], buf[i, cols].reshape(width // 2, qh))
+                acc = term if acc is None else acc + term
+        total[:, n * width // 2 : (n + 1) * width // 2] = acc
+    for j in range(cands):
+        span = pl.ds(j * SEQ, SEQ)
+        here = iota((SEQ, width), 0) == positions[j]
+        out[span] = jnp.where(here, total[rows + j : rows + j + 1], total[span]).astype(BF16)
+
+    for chain in (K1, K2, Q1, Q2, O1, O2, I1, I2, H, M, T):
         chain.finish()
 
     @pl.when(t != y)
@@ -547,15 +583,20 @@
             pltpu.VMEM((Y, Z, depth, qh), BF16),
             pltpu.VMEM((Y, Z, depth, qh), BF16),
             pltpu.VMEM((Y, Z, depth, qh), BF16),
-            pltpu.VMEM((Y, Z, 16, HD), BF16),
+            pltpu.VMEM((Z, 16, HD), BF16),
+            pltpu.VMEM((Y, 16, HD), BF16),
+            pltpu.VMEM((Y, Z * cands, HD), BF16),
+            pltpu.VMEM((Z, Y * cands, HD), BF16),
             pltpu.VMEM((depth, 2 * qh), BF16),
             pltpu.VMEM((cands, HD, HD), BF16),
             pltpu.VMEM((cands, HD, HD), BF16),
             pltpu.VMEM((rows, 2 * HD), F32),
             pltpu.VMEM((rows, group * HD), F32),
             pltpu.VMEM((cands, group * SEQ, HD), BF16),
-            pltpu.VMEM((TP, rows, group * HD), BF16),
-            pltpu.VMEM((rows, width), F32),
+            pltpu.VMEM((TP, rows + 16, group * HD), BF16),
+            pltpu.VMEM((rows + 16, width), F32),
+            pltpu.VMEM((16, HD), F32),
+            pltpu.VMEM((16, HD), F32),
             pltpu.SemaphoreType.DMA((N_SEMS,)),
             pltpu.SemaphoreType.DMA((N_SEMS,)),
             pltpu.SemaphoreType.DMA((6,)),

time: 106 us -> 102 us (0.962)
  Pallas kernels: 104 us -> 99.5 us
    pallas_call x1, Pallas kernels: 104 us -> 99.5 us  [shards(): pl.pallas_call(functools.partial(kernel, (Y, Z, X, TP, cands, group)), ou...]
where the time goes in v3:
time: 102 us; the launch traced here: 101 us
  Pallas kernels  99.5 us (98%)
  local copies, waits for them, and re-layouts  1.77 us (2%)
    pallas_call x1, Pallas kernels, shards(): pl.pallas_call(functools.partial(kernel, (Y, Z, X, TP, cands, group)), ou...  99.5 us

profile of v3, /device:TPU:1, one launch (start us, length us, event | category | flops | bytes accessed | tf_op | source)
XLA Modules:
  0.0 101.3 jit_solution(15130997541608477359)
XLA Ops:
  0.0 99.5 %shard_map.118 = bf16[384,512]{1,0:T(8,128)(2,1)} custom-call(bf16[384,512]{1,0:T(8,128)(2,1)} %hidden.1, f32[1,4096]{1,0:T(1,128)} %bitcast.5, bf16[64,512]{1,0:T(8,128)(2,1)} %w_query.1, bf16[64,128]{1,0:T(8,128)(2,1)} %w_key.1, bf16[64,128]{1,0:T(8,128)(2,1)} %w_value.1, f32[1,128]{1,0:T(1,128)} %bitcast.6, f32[1,128]{1,0:T(1,128)} %bitcast.7, ...), custom_call_target="tpu_custom_call" | custom-call | flops 4000000000 | bytes 2000000 | tf_op jit(solution)/shard_map/pallas_call | solution.py:572
  99.5 1.8 %copy.14 = bf16[384,512]{1,0:T(8,128)(2,1)} copy(bf16[384,512]{1,0:T(8,128)(2,1)} %shard_map.118) | data formatting | bytes 786432

commit v4 on v3

--- a/solution.py
+++ b/solution.py
@@ -118,6 +118,10 @@
     def all(self):
         self.event(*range(self.rounds))
 
+    def relay(self):
+        for ring in self.rings:
+            ring.relay()
+
     def arrive(self):
         for ring in self.rings:
             ring.arrive()
@@ -128,32 +132,55 @@
 
 
 class Direct:
-    def __init__(self, n, me, slot, peer, sems):
-        self.n, self.me, self.slot, self.peer, self.sems = n, me, slot, peer, sems
+    def __init__(self, n, me, slot, peer, sems, sign, relay=False):
+        self.n, self.me, self.slot, self.peer, self.sems, self.sign = n, me, slot, peer, sems, sign
         self.order = sorted(range(1, n), key=lambda d: (min(d, n - d), d))
         self.ids = {d: sems.take() for d in self.order}
-        self.sent = []
-
-    def copy(self, dist, place):
+        self.via = {3: (2, 1), 4: (2, 2), 5: (6, 7)} if relay and n == 8 else {}
+        self.sent, self.relayed = [], False
+
+    def at(self, dist):
+        return lax.rem(self.me + self.sign * dist + self.n, self.n)
+
+    def copy(self, dist, place, hop):
         ref = self.slot(place)
         return pltpu.make_async_remote_copy(
             src_ref=ref,
             dst_ref=ref,
             send_sem=self.sems.send.at[self.ids[dist]],
             recv_sem=self.sems.recv.at[self.ids[dist]],
-            device_id=self.peer(lax.rem(self.me + dist, self.n)),
+            device_id=self.peer(self.at(hop)),
             device_id_type=MESH,
         )
 
+    def send(self, dist, place, hop):
+        copy = self.copy(dist, place, hop)
+        copy.start()
+        self.sent.append(copy)
+
+    def take(self, dist):
+        self.copy(dist, self.at(-dist), dist).wait_recv()
+
     def start(self):
         for dist in reversed(self.order):
-            copy = self.copy(dist, self.me)
-            copy.start()
-            self.sent.append(copy)
+            if dist not in self.via:
+                self.send(dist, self.me, dist)
+
+    def relay(self):
+        for first in sorted({f for f, _ in self.via.values()}):
+            self.take(first)
+            for dist, (source, hop) in self.via.items():
+                if source == first:
+                    self.send(dist, self.at(-first), hop)
+        self.relayed = True
 
     def arrive(self):
+        if not self.relayed:
+            self.relay()
+        firsts = {f for f, _ in self.via.values()}
         for dist in self.order:
-            self.copy(dist, lax.rem(self.me - dist + self.n, self.n)).wait_recv()
+            if dist not in firsts:
+                self.take(dist)
 
     def finish(self):
         for copy in self.sent:
@@ -227,18 +254,25 @@
 def kernel(
     sizes,
     hidden,
-    gain,
+    gain_in,
     w_query,
     w_key,
     w_value,
+    q_gain_in,
+    k_gain_in,
+    w_out,
+    lengths_in,
+    positions_in,
+    cosine_in,
+    sine_in,
+    out,
+    gain,
     q_gain,
     k_gain,
-    w_out,
     lengths,
     positions,
     cosine,
     sine,
-    out,
     hid,
     nrm,
     bk,
@@ -286,6 +320,13 @@
                 (w_query.at[:, pl.ds(0, qh)], bqa.at[y, z]),
                 (w_query.at[:, pl.ds(qh, qh)], bqb.at[y, z]),
                 (w_out, raw),
+                (gain_in, gain),
+                (q_gain_in, q_gain),
+                (k_gain_in, k_gain),
+                (cosine_in, cosine),
+                (sine_in, sine),
+                (lengths_in, lengths),
+                (positions_in, positions),
             ]
         )
     ]
@@ -312,14 +353,16 @@
         pl.semaphore_signal(barrier, inc=1, device_id=peer, device_id_type=MESH)
     pl.semaphore_wait(barrier, len(near))
 
-    def gather(a, b, direct):
+    sign = 1 - 2 * core
+
+    def gather(a, b, direct, relay=False):
         def part(k):
             return pl.ds(k * half, half)
 
         if direct:
             first = Group(
-                Direct(Y, y, lambda i: a.at[i, z], along_y, sems),
-                Direct(Z, z, lambda i: b.at[y, i], along_z, sems),
+                Direct(Y, y, lambda i: a.at[i, z], along_y, sems, sign, relay),
+                Direct(Z, z, lambda i: b.at[y, i], along_z, sems, sign, relay),
             )
         else:
             first = Group(
@@ -336,15 +379,15 @@
     Q1, Q2 = gather(bqa, bqb, True)
     O1, O2 = gather(boa, bob, False)
     I1 = Group(
-        Direct(Z, z, lambda i: key_row.at[i], along_z, sems),
-        Direct(Y, y, lambda i: value_row.at[i], along_y, sems),
+        Direct(Z, z, lambda i: key_row.at[i], along_z, sems, sign),
+        Direct(Y, y, lambda i: value_row.at[i], along_y, sems, sign),
     )
     I2 = Group(
-        Direct(Y, y, lambda i: key_all.at[i], along_y, sems),
-        Direct(Z, z, lambda i: value_all.at[i], along_z, sems),
+        Direct(Y, y, lambda i: key_all.at[i], along_y, sems, sign),
+        Direct(Z, z, lambda i: value_all.at[i], along_z, sems, sign),
     )
     H = ChipGather(X, x, core, cand, hid, rows // 2, sems)
-    T = Direct(TP, t, lambda i: mix.at[i, pl.ds(rows, 16)], along_tp, sems)
+    T = Direct(TP, t, lambda i: mix.at[i, pl.ds(rows, 16)], along_tp, sems, sign)
     M = ChipGather(X, x, core, cand, mix, rows // 2, sems)
 
     fetches[0].wait()
@@ -387,21 +430,25 @@
     K2.start()
     steps(H, 0)
     Q1.arrive()
+    Q2.start()
     K2.event(0, 1)
+    steps(H, 1)
+    Q2.event(0)
+    K2.event(2, 3)
 
     @pl.when(t != y)
     def _():
         for i in range(2):
             swap_copy(i, y).wait_recv()
 
-    steps(H, 1)
-    K2.event(2)
-    Q2.start()
-    K2.event(3, 4)
+    O1.start()
+    Q2.event(1)
     steps(H, 2)
-    O1.start()
-    K2.event(5)
+    K2.event(4, 5)
     H.arrive()
+
+    for fetch in fetches[6:]:
+        fetch.wait()
 
     def squares(i, acc):
         v = hid[i].astype(F32)
@@ -415,10 +462,10 @@
         nrm[:, lanes] = (hid[i].astype(F32) * inverse * gain[:, lanes]).astype(BF16)
         return carry
 
+    Q2.event(2)
     K2.event(6)
     lax.fori_loop(0, TP, scale, 0)
-    Q2.event(0)
-    O1.event(0)
+    O1.event(0, 1)
 
     def norm_rope(v, weight):
         v = v * lax.rsqrt(jnp.mean(v * v, axis=-1, keepdims=True) + EPSILON) * weight
@@ -426,8 +473,8 @@
 
     kacc[:, :HD] = dot(nrm[...], bk[...].reshape(TP * width, HD))
     kacc[:, HD:] = dot(nrm[...], bv[...].reshape(TP * width, HD))
-    Q2.event(1)
-    O1.event(1, 2)
+    Q2.event(3)
+    O1.event(2, 3)
     pad = jnp.zeros((HD - SEQ, HD), BF16)
     picked = [jnp.zeros((16, HD), F32)] * 2
     for j in range(cands):
@@ -442,9 +489,8 @@
     key_row[z] = picked[0].astype(BF16)
     value_row[y] = picked[1].astype(BF16)
     I1.start()
-    Q2.event(2)
-    O1.event(3, 4, 5, 6)
-    Q2.event(3, 4)
+    Q2.event(4)
+    O1.event(4, 5, 6)
     O2.start()
     Q2.event(5, 6)
     I1.arrive()
@@ -456,7 +502,6 @@
     I2.start()
 
     qacc[:, :qh] = dot(nrm[...], bqa[...].reshape(TP * width, qh))
-    O2.event(0)
     qacc[:, qh:] = dot(nrm[...], bqb[...].reshape(TP * width, qh))
     asked = jnp.zeros((16, HD), F32)
     for j in range(cands):
@@ -468,8 +513,6 @@
         h = iota(shape, 0) - group * j
         here = (h >= 0) & (h < group) & (iota(shape, 1) == h * SEQ + positions[j])
         asked += dot(jnp.where(here, 1.0, 0.0).astype(BF16), qbuf[j])
-    O2.event(1)
-
     factor = float(HD) ** (-0.5)
     slot_s, slot_t = iota((SEQ, HD), 0), iota((SEQ, HD), 1)
     for j in range(cands):
@@ -488,11 +531,11 @@
             mix[t, pl.ds(j * SEQ, SEQ), pl.ds(h * HD, HD)] = (num[span] / den[span]).astype(BF16)
         if j == cands // 2 - 1:
             M.start(0)
+            O2.event(0)
     M.start(1)
-    O2.event(2)
+    O2.event(1, 2)
+    steps(M, 0)
     O2.event(3)
-    steps(M, 0)
-    O2.event(4)
     I2.arrive()
 
     count = Y * Z * cands
@@ -517,6 +560,7 @@
         sel = jnp.where((row < cands) & (column == row * group + h), 1.0, 0.0).astype(BF16)
         mix[t, pl.ds(rows, 16), pl.ds(h * HD, HD)] = dot(sel, mixed).astype(BF16)
     T.start()
+    O2.event(4)
     steps(M, 1)
     O2.event(5)
     steps(M, 2)
@@ -566,15 +610,20 @@
     cands, group = rows // SEQ, w_query.shape[1] // w_key.shape[1]
     qh = group * HD // 2
     cosine, sine = rope_tables()
-    any_, vmem, smem = (
-        pl.BlockSpec(memory_space=m) for m in (pl.ANY, pltpu.VMEM, pltpu.SMEM)
-    )
+    any_, vmem = (pl.BlockSpec(memory_space=m) for m in (pl.ANY, pltpu.VMEM))
     return pl.pallas_call(
         functools.partial(kernel, (Y, Z, X, TP, cands, group)),
         out_shape=jax.ShapeDtypeStruct((rows, width), BF16),
-        in_specs=[any_, vmem, any_, any_, any_, vmem, vmem, any_, smem, smem, vmem, vmem],
+        in_specs=[any_] * 12,
         out_specs=vmem,
         scratch_shapes=[
+            pltpu.VMEM((1, TP * width), F32),
+            pltpu.VMEM((1, HD), F32),
+            pltpu.VMEM((1, HD), F32),
+            pltpu.SMEM(lengths.shape, jnp.int32),
+            pltpu.SMEM(positions.shape, jnp.int32),
+            pltpu.VMEM((SEQ, HD), F32),
+            pltpu.VMEM((SEQ, HD), F32),
             pltpu.VMEM((TP, rows, width), BF16),
             pltpu.VMEM((rows, TP * width), BF16),
             pltpu.VMEM((Y, Z, depth, HD), BF16),
@@ -599,7 +648,7 @@
             pltpu.VMEM((16, HD), F32),
             pltpu.SemaphoreType.DMA((N_SEMS,)),
             pltpu.SemaphoreType.DMA((N_SEMS,)),
-            pltpu.SemaphoreType.DMA((6,)),
+            pltpu.SemaphoreType.DMA((13,)),
         ],
         compiler_params=pltpu.CompilerParams(
             collective_id=0, has_side_effects=True, vmem_limit_bytes=56 * 1024 * 1024

time: 102 us -> 96 us (0.941)
  Pallas kernels: 99.5 us -> 93.3 us
    pallas_call x1, Pallas kernels: 99.5 us -> 93.3 us  [shards(): pl.pallas_call(functools.partial(kernel, (Y, Z, X, TP, cands, group)), ou...]
where the time goes in v4:
time: 96 us; the launch traced here: 95.1 us
  Pallas kernels  93.3 us (97%)
  local copies, waits for them, and re-layouts  1.77 us (2%)
    pallas_call x1, Pallas kernels, shards(): pl.pallas_call(functools.partial(kernel, (Y, Z, X, TP, cands, group)), ou...  93.3 us

profile of v4, /device:TPU:1, one launch (start us, length us, event | category | flops | bytes accessed | tf_op | source)
XLA Modules:
  0.0 95.1 jit_solution(17332360914488313238)
XLA Ops:
  0.0 93.3 %shard_map.118 = bf16[384,512]{1,0:T(8,128)(2,1)} custom-call(bf16[384,512]{1,0:T(8,128)(2,1)} %hidden.1, f32[1,4096]{1,0:T(1,128)} %bitcast.5, bf16[64,512]{1,0:T(8,128)(2,1)} %w_query.1, bf16[64,128]{1,0:T(8,128)(2,1)} %w_key.1, bf16[64,128]{1,0:T(8,128)(2,1)} %w_value.1, f32[1,128]{1,0:T(1,128)} %bitcast.6, f32[1,128]{1,0:T(1,128)} %bitcast.7, ...), custom_call_target="tpu_custom_call" | custom-call | flops 4000000000 | bytes 2000000 | tf_op jit(solution)/shard_map/pallas_call | solution.py:614
  93.3 1.8 %copy.14 = bf16[384,512]{1,0:T(8,128)(2,1)} copy(bf16[384,512]{1,0:T(8,128)(2,1)} %shard_map.118) | data formatting | bytes 786432

commit v5 on v4

--- a/solution.py
+++ b/solution.py
@@ -393,11 +393,11 @@
     fetches[0].wait()
     fetches[1].wait()
     K1.start()
-    fetches[2].wait()
-    H.start()
     fetches[3].wait()
     fetches[4].wait()
     Q1.start()
+    fetches[2].wait()
+    H.start()
 
     fetches[5].wait()
     swaps = [sems.take(), sems.take()]
@@ -489,10 +489,12 @@
     key_row[z] = picked[0].astype(BF16)
     value_row[y] = picked[1].astype(BF16)
     I1.start()
+    O1.event(4, 5)
     Q2.event(4)
-    O1.event(4, 5, 6)
+    O1.event(6)
+    Q2.event(5)
     O2.start()
-    Q2.event(5, 6)
+    Q2.event(6)
     I1.arrive()
     for n, me, rows_of, block in ((Z, y, key_row, key_all), (Y, z, value_row, value_all)):
         shape = (n * cands, n * 16)

time: 96 us -> 95.3 us (level)
  no operation moved by 1% of the time
where the time goes in v5:
time: 95.3 us; the launch traced here: 95 us
  Pallas kernels  93.2 us (98%)
  local copies, waits for them, and re-layouts  1.77 us (2%)
    pallas_call x1, Pallas kernels, shards(): pl.pallas_call(functools.partial(kernel, (Y, Z, X, TP, cands, group)), ou...  93.2 us

profile of v5, /device:TPU:1, one launch (start us, length us, event | category | flops | bytes accessed | tf_op | source)
XLA Modules:
  0.0 95.0 jit_solution(2247752284321160797)
XLA Ops:
  0.0 93.2 %shard_map.118 = bf16[384,512]{1,0:T(8,128)(2,1)} custom-call(bf16[384,512]{1,0:T(8,128)(2,1)} %hidden.1, f32[1,4096]{1,0:T(1,128)} %bitcast.5, bf16[64,512]{1,0:T(8,128)(2,1)} %w_query.1, bf16[64,128]{1,0:T(8,128)(2,1)} %w_key.1, bf16[64,128]{1,0:T(8,128)(2,1)} %w_value.1, f32[1,128]{1,0:T(1,128)} %bitcast.6, f32[1,128]{1,0:T(1,128)} %bitcast.7, ...), custom_call_target="tpu_custom_call" | custom-call | flops 4000000000 | bytes 2000000 | tf_op jit(solution)/shard_map/pallas_call | solution.py:616
  93.2 1.8 %copy.14 = bf16[384,512]{1,0:T(8,128)(2,1)} copy(bf16[384,512]{1,0:T(8,128)(2,1)} %shard_map.118) | data formatting | bytes 786432
